TPU v7x, 32 devices: a whole 2x2x4 slice. The times are simulated.
32 devices in a mesh: pix: 4 (over z), cell: 8 (over y, x, core).
Axes of the slice: x: 2, y: 2, z: 4, core: 2. Of those that a mesh axis runs over, the one named last changes fastest.
Arguments:
- influence: float32 [32768, 16384], P('pix', 'cell'), as said below
- observed: float32 [32768, 128], P(('pix', 'cell')), may hold values from -6 to 6
Outputs:
- power: float32 [16384, 128], P(('cell', 'pix'))
- residual: float32 [32768, 128], P(('pix', 'cell'))
- gradient: float32 [16384, 128], P(('cell', 'pix'))
Inputs may be any that keep to these rules, and one draw needn't show every extreme that they name: A dense influence matrix with independent entries.
All inputs are finite; a program needn't handle non-finite values.
Results may differ from a plain program's by a relative error of at most 0.0003.
Values sent between devices are 32-bit elements; how exact they have to be, the bound alone decides.
No kernel may reach another device: no remote copies, remote signals or barrier semaphores. Data moves between devices by JAX's collectives and lax.ppermute only.
A program may use at most 128 MiB of HBM per device.

v0:
```python
import functools

import jax
import jax.numpy as jnp
from jax import lax
from jax.experimental import pallas as pl
from jax.experimental.pallas import tpu as pltpu
from jax.sharding import PartitionSpec as P

ITERS = 2
BLOCK_ROWS = 512
FIRST_LIMIT = 18 * 2**20
LATER_LIMIT = 9 * 2**20
f32 = jnp.float32
bf16 = jnp.bfloat16
f8 = jnp.float8_e4m3fn
RANGE = 224.0 * 256.0
VMEM = pl.BlockSpec(memory_space=pltpu.VMEM)
SMEM = pl.BlockSpec(memory_space=pltpu.SMEM)


def resident(x):
    return pltpu.with_memory_space_constraint(x, pltpu.VMEM)


def split(x):
    high = x.astype(bf16)
    return high, (x - high.astype(f32)).astype(bf16)


def squares(x):
    return jnp.sum(x * x, axis=0, keepdims=True)


def cost(rows, cols, frames, width):
    return pl.CostEstimate(flops=2 * 3 * rows * cols * frames, bytes_accessed=width * rows * cols, transcendentals=0)


def emit_parts(pix, acc, sums, flat_ref, out_ref):
    parts = out_ref.shape[0]
    cells = out_ref.shape[1] - 8
    flat_ref[...] = acc.T
    for part in range(parts):
        start = pl.multiple_of(((pix & (parts - 1)) ^ part) * cells, cells)
        out_ref[part, :cells, :] = flat_ref[pl.ds(start, cells), :]
        out_ref[part, cells:, :] = sums


def first_kernel(count, per_chunk, first, last, index_ref, *refs):
    r_refs, refs = refs[:count], refs[count:]
    near_ref, far_ref, refs = refs[0], refs[1], refs[2:]
    if not first:
        (near_in, far_in, sum_in), refs = refs[:3], refs[3:]
    high_refs, low_refs, scale_ref, refs = refs[:2], refs[2:4], refs[4], refs[5:]
    if last:
        near_out, far_out, near, far, sums, cat_ref, flat_ref = refs
    else:
        near, far, sums, cat_ref = refs
    step = pl.program_id(0)
    frames = r_refs[0].shape[1]
    rows, half = near_ref.shape

    @pl.when(step == 0)
    def _():
        total = jnp.zeros((1, frames), f32)
        for i in range(count):
            r = r_refs[i][...]
            total = total + squares(r)
            for k in range(per_chunk):
                high, low = split(r[k * rows : (k + 1) * rows].T)
                cat_ref[i * per_chunk + k, :frames, :] = high
                cat_ref[i * per_chunk + k, frames:, :] = low
        if first:
            sums[...] = jnp.broadcast_to(total, sums.shape)
            near[...] = jnp.zeros_like(near)
            far[...] = jnp.zeros_like(far)
        else:
            sums[...] = sum_in[...] + total
            near[...] = near_in[...]
            far[...] = far_in[...]

    here = pl.ds(pl.multiple_of(step * rows, rows), rows)
    for k, (ref, acc) in enumerate(((near_ref, near), (far_ref, far))):
        high, low = split(ref[...])
        high_refs[k][here, :] = high
        both = jnp.dot(cat_ref[step], high, preferred_element_type=f32)
        other = jnp.dot(cat_ref[step, :frames, :], low, preferred_element_type=f32)
        largest = jnp.maximum(jnp.max(jnp.max(jnp.abs(high), axis=0, keepdims=True).astype(f32)), 1e-30)
        low_refs[k][...] = (low * (RANGE / largest).astype(bf16)).astype(f8)
        scale_ref[step, k] = largest * (1.0 / RANGE)
        acc[...] += both[:frames] + both[frames:] + other

    if last:

        @pl.when(step == count * per_chunk - 1)
        def _():
            emit_parts(index_ref[0], near[...], sums[...], flat_ref, near_out)
            emit_parts(index_ref[0], far[...], sums[...], flat_ref, far_out)


def blocks(rows, half, per_chunk, base):
    def block(far):
        def where(s, ix):
            return (ix[2 + base + s // per_chunk] * per_chunk + s % per_chunk, ix[1] ^ far)

        return pl.BlockSpec((rows, half), where)

    return [block(0), block(1)]


def first_call(influence, r_parts, index, base, carry, last, parts):
    count = len(r_parts)
    cols = influence.shape[1]
    half = cols // 2
    chunk_rows, frames = r_parts[0].shape
    rows = min(BLOCK_ROWS, chunk_rows)
    per_chunk = chunk_rows // rows
    accs = [((frames, half), f32)] * 2 + [((8, frames), f32)]
    cat = pltpu.VMEM((count * per_chunk, 2 * frames, rows), bf16)
    out_shape = [
        *[pltpu.VMEM((count * chunk_rows, half), bf16)] * 2,
        *[pltpu.HBM((count * chunk_rows, half), f8)] * 2,
        jax.ShapeDtypeStruct((count * per_chunk, 2), f32),
    ]
    if last:
        out_shape += [jax.ShapeDtypeStruct((parts // 2, half // (parts // 2) + 8, frames), f32)] * 2
        scratch = [pltpu.VMEM(*a) for a in accs] + [cat, pltpu.VMEM((half, frames), f32)]
    else:
        out_shape += [jax.ShapeDtypeStruct(*a) for a in accs]
        scratch = [cat]
    high_near, high_far, low_near, low_far, scale, *rest = pl.pallas_call(
        functools.partial(first_kernel, count, per_chunk, carry is None, last),
        grid_spec=pltpu.PrefetchScalarGridSpec(
            num_scalar_prefetch=1,
            grid=(count * per_chunk,),
            in_specs=[VMEM] * count + blocks(rows, half, per_chunk, base) + [VMEM] * (0 if carry is None else 3),
            out_specs=[VMEM] * 2 + [pl.BlockSpec((rows, half), lambda s, ix: (s, 0))] * 2 + [SMEM] + [VMEM] * (len(out_shape) - 5),
            scratch_shapes=scratch,
        ),
        out_shape=out_shape,
        compiler_params=pltpu.CompilerParams(vmem_limit_bytes=FIRST_LIMIT),
        cost_estimate=cost(count * chunk_rows, cols, frames, 4),
        name="first_adjoint",
    )(index, *r_parts, influence, influence, *(() if carry is None else carry))
    return (high_near, high_far), (low_near, low_far, scale), rest


def adjoint_kernel(count, sides, last, index_ref, *refs):
    halves = len(sides)
    r_refs, refs = refs[:count], refs[count:]
    high_refs, low_refs, scale_ref, refs = refs[:halves], refs[halves : 2 * halves], refs[2 * halves], refs[2 * halves + 1 :]
    accs_in, sum_in, refs = refs[:halves], refs[halves], refs[halves + 1 :]
    if last:
        outs, refs = refs[:1], refs[1:]
    else:
        outs, sum_out, refs = refs[:halves], refs[halves], refs[halves + 1 :]
    cat_ref, scaled_ref = refs[:2]
    chunk_rows, frames = r_refs[0].shape
    rows = cat_ref.shape[1] // scale_ref.shape[0]
    total = sum_in[...]
    for i in range(count):
        r = r_refs[i][...]
        total = total + squares(r)
        turned = r.T
        high, low = split(turned)
        here = slice(i * chunk_rows, (i + 1) * chunk_rows)
        cat_ref[:frames, here] = high
        cat_ref[frames:, here] = low
        for b in range(chunk_rows // rows):
            at = i * chunk_rows + b * rows
            for k in range(halves):
                scale = scale_ref[at // rows, sides[k]]
                scaled_ref[k, :, at : at + rows] = (turned[:, b * rows : (b + 1) * rows] * scale).astype(bf16)
    for k in range(halves):
        both = jnp.dot(cat_ref[...], high_refs[k][...], preferred_element_type=f32)
        acc = accs_in[k][...] + both[:frames] + both[frames:]
        acc = acc + jnp.dot(scaled_ref[k], low_refs[k][...].astype(bf16), preferred_element_type=f32)
        if last:
            emit_parts(index_ref[0], acc, total, refs[2], outs[0])
        else:
            outs[k][...] = acc
    if not last:
        sum_out[...] = total


def adjoint_call(high, low, r_parts, index, carry, sides, last, parts):
    count = len(r_parts)
    rows = high[0].shape[0]
    halves = len(sides)
    half = carry[0].shape[1]
    frames = r_parts[0].shape[1]
    scratch = [
        pltpu.VMEM((2 * frames, rows), bf16),
        pltpu.VMEM((halves, frames, rows), bf16),
    ]
    if last:
        out_shape = jax.ShapeDtypeStruct((parts // 2, half // (parts // 2) + 8, frames), f32)
        out_specs = VMEM
        scratch.append(pltpu.VMEM((half, frames), f32))
    else:
        out_shape = [jax.ShapeDtypeStruct(c.shape, f32) for c in carry]
        out_specs = [VMEM] * (halves + 1)
    return pl.pallas_call(
        functools.partial(adjoint_kernel, count, sides, last),
        in_specs=[SMEM] + [VMEM] * (count + 2 * halves) + [SMEM] + [VMEM] * (halves + 1),
        out_specs=out_specs,
        out_shape=out_shape,
        scratch_shapes=scratch,
        compiler_params=pltpu.CompilerParams(vmem_limit_bytes=LATER_LIMIT),
        cost_estimate=cost(rows, halves * half, frames, 2),
        name="adjoint_product",
    )(
        index,
        *r_parts,
        *[resident(high[k]) for k in sides],
        *[resident(low[k]) for k in sides],
        low[2],
        *carry,
    )


def forward_kernel(parts, arrays, places, side, chunk_rows, near, index_ref, *refs):
    x_refs, refs = refs[:parts], refs[parts:]
    highs, lows, scales, refs = refs[:arrays], refs[arrays : 2 * arrays], refs[2 * arrays : 3 * arrays], refs[3 * arrays :]
    count = len(places)
    if not near:
        added, sum_in, refs = refs[:count], refs[count], refs[count + 1 :]
    if near:
        outs, sum_out, refs = refs[:count], refs[count], refs[count + 1 :]
    else:
        outs, refs = [refs[0].at[i] for i in range(count)], refs[1:]
    (cat_ref,) = refs
    cells, frames = x_refs[0].shape
    total = jnp.zeros((1, frames), f32)
    for part in range(parts):
        x = x_refs[part][...]
        high, low = split(x)
        start = pl.multiple_of(((index_ref[0] & (parts - 1)) ^ part) * cells, cells)
        cat_ref[pl.ds(start, cells), :frames] = high
        cat_ref[pl.ds(start, cells), frames:] = low
        total = total + squares(x)
    if near:
        sum_out[...] = jnp.broadcast_to(total, sum_out.shape)
    for i, (which, row) in enumerate(places):
        both = jnp.dot(highs[which][row : row + chunk_rows, :], cat_ref[...], preferred_element_type=f32)
        value = both[:, :frames] + both[:, frames:]
        other = jnp.dot(lows[which][row : row + chunk_rows, :].astype(bf16), cat_ref[:, :frames], preferred_element_type=f32)
        rows = highs[which].shape[0] // scales[which].shape[0]
        for start in range(0, chunk_rows, rows):
            at = slice(start, start + rows)
            whole = value[at] + other[at] * scales[which][(row + start) // rows, side]
            outs[i][at, :] = whole if near else whole + added[i][at, :]
        if not near:
            outs[i][chunk_rows:, :] = sum_in[...] + total


def forward_call(highs, lows, x_parts, index, places, chunk_rows, side, added):
    count = len(places)
    used = sorted({g for g, _ in places})
    slots = [(used.index(g), row) for g, row in places]
    cells, frames = x_parts[0].shape
    half = cells * len(x_parts)
    near = added is None
    extra = [] if near else [*added[0], added[1]]
    rows = chunk_rows if near else chunk_rows + 8
    if near:
        out_shape = [jax.ShapeDtypeStruct((rows, frames), f32)] * count + [jax.ShapeDtypeStruct((8, frames), f32)]
    else:
        out_shape = [jax.ShapeDtypeStruct((count, rows, frames), f32)]
    result = pl.pallas_call(
        functools.partial(forward_kernel, len(x_parts), len(used), slots, side, chunk_rows, near),
        in_specs=[SMEM]
        + [VMEM] * (len(x_parts) + len(used))
        + [VMEM] * len(used)
        + [SMEM] * len(used)
        + [VMEM] * len(extra),
        out_specs=[VMEM] * len(out_shape),
        out_shape=out_shape,
        scratch_shapes=[
            pltpu.VMEM((half, 2 * frames), bf16),
        ],
        compiler_params=pltpu.CompilerParams(vmem_limit_bytes=LATER_LIMIT),
        cost_estimate=cost(count * chunk_rows, half, frames, 2),
        name="forward_product",
    )(
        index,
        *x_parts,
        *[resident(highs[g][side]) for g in used],
        *[resident(lows[g][side]) for g in used],
        *[lows[g][2] for g in used],
        *extra,
    )
    return result if near else result[0]


def solution(mesh):
    cell_size, pix_size = mesh.shape["cell"], mesh.shape["pix"]
    bits = cell_size.bit_length() - 1
    stages = bits - 1
    group = cell_size // 2
    order = (list(range(1, bits)), list(range(bits - 1, 0, -1)))

    def offset(core, w):
        return sum(1 << order[core][j] for j in range(stages) if (w >> (stages - 1 - j)) & 1)

    stage_perm = [[(i, i ^ (1 << order[i & 1][j])) for i in range(cell_size)] for j in range(stages)]
    core_perm = [(i, i ^ 1) for i in range(cell_size)]
    pix_bits = pix_size.bit_length() - 1
    pix_perm = [[(i, i ^ (1 << b)) for i in range(pix_size)] for b in range(pix_bits)]
    middle = range(1, group - 1)
    groups = [[(0, 0), (1, 0)], [(0, w) for w in middle], [(1, w) for w in middle], [(0, group - 1), (1, group - 1)]]

    starts = [sum(map(len, groups[:g])) for g in range(len(groups))]
    uses = [[offset(core ^ c, w) ^ c for members in groups for c, w in members] for core in range(2)]

    def body(influence, observed):
        chunk_rows = influence.shape[0] // cell_size
        me_cell, me_pix = lax.axis_index("cell"), lax.axis_index("pix")
        order_of_use = jnp.where((me_cell & 1) == 0, jnp.array(uses[0], jnp.int32), jnp.array(uses[1], jnp.int32))
        index = jnp.concatenate([jnp.stack([me_pix, me_pix // (pix_size // 2)]), me_cell ^ order_of_use])
        place = {c: (g, i * chunk_rows) for g, members in enumerate(groups) for i, c in enumerate(members)}
        highs, lows = [], []

        def stage(piece, j):
            return lax.ppermute(piece, "cell", stage_perm[j])

        def flip(piece):
            return lax.ppermute(piece, "cell", core_perm)

        def between(piece, b):
            return lax.ppermute(piece, "pix", pix_perm[b])

        def adjoint(residual):
            half = influence.shape[1] // 2
            first = not highs
            carry = None if first else [
                jnp.zeros((residual.shape[1], half), f32),
                jnp.zeros((residual.shape[1], half), f32),
                jnp.zeros((8, residual.shape[1]), f32),
            ]

            def multiply(g, pieces, carry):
                if first:
                    high, low, carry = first_call(
                        influence, pieces, index, starts[g], carry, g == len(groups) - 1, pix_size
                    )
                    highs.append(high)
                    lows.append(low)
                    return carry
                return adjoint_call(highs[g], lows[g], pieces, index, carry, (0, 1), False, pix_size)

            def finish(pieces, carry, side):
                carry = adjoint_call(highs[2], lows[2], pieces[0], index, carry, (side,), False, pix_size)
                return adjoint_call(highs[3], lows[3], pieces[1], index, carry, (side,), True, pix_size)

            mine = [residual]
            for j in reversed(range(1, stages)):
                mine = mine + [stage(piece, j) for piece in mine]
            early = stage(residual, 0) if first else None
            carry = multiply(0, [residual, flip(residual)], carry)
            late, carry = lax.optimization_barrier((residual, carry))
            crossed = early if first else stage(late, 0)
            rest, carry = lax.optimization_barrier((mine[1:], carry))
            mine = [residual, *rest, crossed, *[stage(piece, 0) for piece in rest]]
            theirs = [None] + [flip(piece) for piece in mine[1 : group - 1]]
            carry = multiply(1, [mine[w] for w in middle], carry)
            last, carry = lax.optimization_barrier((mine[group - 1], carry))
            pieces = [theirs[w] for w in middle], [last, flip(last)]
            if first:
                near, far = multiply(3, pieces[1], multiply(2, pieces[0], carry))
            else:
                far = finish(pieces, [carry[1], carry[2]], 1)
                far, carry = lax.optimization_barrier((far, carry))
                near = finish(pieces, [carry[0], carry[2]], 0)
            held = [near[l] for l in range(pix_size // 2)] + [far[l] for l in range(pix_size // 2)]
            for b in range(pix_bits):
                arrived = None
                for l in reversed([l for l in range(0, pix_size, 1 << b) if l >> b & 1]):
                    piece = held[l]
                    if arrived is not None:
                        piece, arrived = lax.optimization_barrier((piece, arrived))
                        held[l_before ^ 1 << b] = held[l_before ^ 1 << b] + arrived
                    arrived, l_before = between(piece, b), l
                held[l_before ^ 1 << b] = held[l_before ^ 1 << b] + arrived
            return held[0][:-8], held[0][-8]

        def forward(gradient):
            def spread(piece):
                known = {0: piece}
                for b in reversed(range(pix_bits - 1)):
                    for l in list(known):
                        known[l ^ 1 << b] = between(known[l], b)
                return [known[l] for l in range(pix_size // 2)]

            across = between(gradient, pix_bits - 1)
            near = spread(gradient)
            theirs = [place[1, w] for w in range(group)]
            mine = [place[0, w] for w in range(group)]
            *their_near, sums = forward_call(highs, lows, near, index, theirs, chunk_rows, 0, None)
            across, near, their_near = lax.optimization_barrier((across, near, their_near))
            far = spread(across)
            *mine_near, _ = forward_call(highs, lows, near, index, mine, chunk_rows, 0, None)
            half = group // 2
            far, mine_near = lax.optimization_barrier((far, mine_near))

            def finish(far, places, added):
                return forward_call(highs, lows, far, index, places, chunk_rows, 1, (added, sums))

            away, home = slice(half, group), slice(0, half)
            sent_away = flip(finish(far, theirs[away], their_near[away]))
            kept_away = finish(far, mine[away], mine_near[away])
            far, kept_away = lax.optimization_barrier((far, kept_away))
            sent_home = flip(finish(far, theirs[home], their_near[home]))
            kept_home = finish(far, mine[home], mine_near[home])
            held = [kept_home[w] + sent_home[w] for w in range(half)]
            held += [kept_away[w] + sent_away[w] for w in range(group - half)]
            for j in range(stages):
                half = len(held) // 2
                for w in reversed(range(half)):
                    held[w] = held[w] + stage(held[w + half], j)
                held = held[:half]
            return held[0][:-8], held[0][-8]

        gradient, _ = adjoint(observed)
        image, gamma = forward(gradient)
        direction = gradient
        residual = observed
        power = jnp.zeros_like(gradient)
        for step in range(ITERS):
            back, image_squares = adjoint(image)
            alpha = gamma / image_squares
            power = power + alpha * direction
            residual = residual - alpha * image
            gradient = gradient - alpha * back
            if step + 1 < ITERS:
                fresh_image, fresh = forward(gradient)
                beta = fresh / gamma
                image = fresh_image + beta * image
                direction = gradient + beta * direction
                gamma = fresh
        return (power, residual, gradient)

    in_specs = (P("pix", "cell"), P(("pix", "cell"), None))
    out_specs = (P(("cell", "pix"), None), P(("pix", "cell"), None), P(("cell", "pix"), None))
    return jax.shard_map(body, mesh=mesh, in_specs=in_specs, out_specs=out_specs, check_vma=False)
```

profile of v0, /device:TPU:0, one launch (start us, length us, event | category | flops | bytes accessed | tf_op | source)
XLA Modules:
  0.0 294.0 jit_solution(13764021376927258536)
XLA Ops:
  7.0 11.0 %first_adjoint.4 = (bf16[2048,1024]{1,0:T(8,128)(2,1)S(1)}, bf16[2048,1024]{1,0:T(8,128)(2,1)S(1)}, f8e4m3fn[2048,1024]{1,0:T(32,128)(4,1)}, f8e4m3fn[2048,1024]...) custom-call(s32[10]{0:T(128)S(1)} %pad_add_fusion.index_ref, ...), custom_call_target="tpu_custom_call" | custom-call | flops 3221225472 | bytes 16777216 | tf_op jit(solution)/shard_map/first_adjoint/pallas_call | solution.py:131
  19.1 11.2 %first_adjoint.5 = (bf16[2048,1024]{1,0:T(8,128)(2,1)S(1)}, bf16[2048,1024]{1,0:T(8,128)(2,1)S(1)}, f8e4m3fn[2048,1024]{1,0:T(32,128)(4,1)}, f8e4m3fn[2048,1024]...) custom-call(s32[10]{0:T(128)S(1)} %pad_add_fusion.index_ref, ...), custom_call_target="tpu_custom_call" | custom-call | flops 3221225472 | bytes 16777216 | tf_op jit(solution)/shard_map/first_adjoint/pallas_call | solution.py:131
  30.3 11.7 %first_adjoint.6 = (bf16[2048,1024]{1,0:T(8,128)(2,1)S(1)}, bf16[2048,1024]{1,0:T(8,128)(2,1)S(1)}, f8e4m3fn[2048,1024]{1,0:T(32,128)(4,1)}, f8e4m3fn[2048,1024]...) custom-call(s32[10]{0:T(128)S(1)} %pad_add_fusion.index_ref, ...), custom_call_target="tpu_custom_call" | custom-call | flops 3221225472 | bytes 16777216 | tf_op jit(solution)/shard_map/first_adjoint/pallas_call | solution.py:131
  42.1 13.8 %first_adjoint.7 = (bf16[2048,1024]{1,0:T(8,128)(2,1)S(1)}, bf16[2048,1024]{1,0:T(8,128)(2,1)S(1)}, f8e4m3fn[2048,1024]{1,0:T(32,128)(4,1)}, f8e4m3fn[2048,1024]...) custom-call(s32[10]{0:T(128)S(1)} %pad_add_fusion.index_ref, ...), custom_call_target="tpu_custom_call" | custom-call | flops 3221225472 | bytes 16777216 | tf_op jit(solution)/shard_map/first_adjoint/pallas_call | solution.py:131
  57.7 6.6 %collective-permute-done.7 = f32[520,128]{1,0:T(8,128)S(1)} collective-permute-done((f32[520,128]{1,0:T(8,128)S(1)}, f32[520,128]{1,0:T(8,128)S(1)}, u32[]{:S(2)}, u32[]{:S(2)}) %collective-permute-start.7) | collective-permute-done | bytes 266272 | tf_op jit(solution)/shard_map/ppermute | solution.py:331
  68.6 9.9 %collective-permute-done.9 = f32[520,128]{1,0:T(8,128)S(1)} collective-permute-done((f32[520,128]{1,0:T(8,128)S(1)}, f32[520,128]{1,0:T(8,128)S(1)}, u32[]{:S(2)}, u32[]{:S(2)}) %collective-permute-start.9) | collective-permute-done | bytes 266272 | tf_op jit(solution)/shard_map/ppermute | solution.py:331
  82.6 8.5 %collective-permute-done.11.refs_1_ = f32[512,128]{1,0:T(8,128)S(1)} collective-permute-done((f32[512,128]{1,0:T(8,128)S(1)}, f32[512,128]{1,0:T(8,128)S(1)}, u32[]{:S(2)}, u32[]{:S(2)}) %collective-permute-start.11) | collective-permute-done | bytes 262176 | tf_op jit(solution)/shard_map/ppermute | solution.py:331
  91.1 5.3 %forward_product.12 = (f32[1024,128]{1,0:T(8,128)S(1)}, f32[1024,128]{1,0:T(8,128)S(1)}, f32[1024,128]{1,0:T(8,128)S(1)}, f32[1024,128]{1,0:T(8,128)S(1)}, f32[8,128]{1,0:T(8,128)S(1)}) custom-call(s32[10]{0:T(128)S(1)} %pad_add_fusion.index_ref, f32[512,128]{1,0:T(8,128)S(1)} %slice_add_fusion.9.refs_0_, f32[512,128]{1,0:T(8,128)S(1)} %collective-permute-done.11.refs_1_, ...), custom_call_target="tpu_custom_call" | custom-call | flops 3221225472 | bytes 8388608 | tf_op jit(solution)/shard_map/forward_product/pallas_call | solution.py:270
  96.5 5.8 %forward_product.13 = (f32[1024,128]{1,0:T(8,128)S(1)}, f32[1024,128]{1,0:T(8,128)S(1)}, f32[1024,128]{1,0:T(8,128)S(1)}, f32[1024,128]{1,0:T(8,128)S(1)}, f32[8,128]{1,0:T(8,128)}) custom-call(s32[10]{0:T(128)S(1)} %pad_add_fusion.index_ref, f32[512,128]{1,0:T(8,128)S(1)} %slice_add_fusion.9.refs_0_, f32[512,128]{1,0:T(8,128)S(1)} %collective-permute-done.11.refs_1_, ...), custom_call_target="tpu_custom_call" | custom-call | flops 3221225472 | bytes 8388608 | tf_op jit(solution)/shard_map/forward_product/pallas_call | solution.py:270
  102.9 3.1 %forward_product.17 = f32[2,1032,128]{2,1,0:T(8,128)S(1)} custom-call(s32[10]{0:T(128)S(1)} %pad_add_fusion.index_ref, f32[512,128]{1,0:T(8,128)S(1)} %collective-permute-done.10.refs_0_, f32[512,128]{1,0:T(8,128)S(1)} %collective-permute-done.12.refs_1_, bf16[2048,1024]{1,0:T(8,128)(2,1)S(1)} %get-tuple-element.213.refs_3_.refs_2_, ...), custom_call_target="tpu_custom_call" | custom-call | flops 1610612736 | bytes 4194304 | tf_op jit(solution)/shard_map/forward_product/pallas_call | solution.py:270
  106.1 3.1 %forward_product.14 = f32[2,1032,128]{2,1,0:T(8,128)S(1)} custom-call(s32[10]{0:T(128)S(1)} %pad_add_fusion.index_ref, f32[512,128]{1,0:T(8,128)S(1)} %collective-permute-done.10.refs_0_, f32[512,128]{1,0:T(8,128)S(1)} %collective-permute-done.12.refs_1_, bf16[2048,1024]{1,0:T(8,128)(2,1)S(1)} %get-tuple-element.200.refs_2_.refs_3_, ...), custom_call_target="tpu_custom_call" | custom-call | flops 1610612736 | bytes 4194304 | tf_op jit(solution)/shard_map/forward_product/pallas_call | solution.py:270
  109.2 3.5 %forward_product.16 = f32[2,1032,128]{2,1,0:T(8,128)S(1)} custom-call(s32[10]{0:T(128)S(1)} %pad_add_fusion.index_ref, f32[512,128]{1,0:T(8,128)S(1)} %collective-permute-done.10.refs_0_, f32[512,128]{1,0:T(8,128)S(1)} %collective-permute-done.12.refs_1_, bf16[2048,1024]{1,0:T(8,128)(2,1)S(1)} %get-tuple-element.209.refs_2_.refs_3_, ...), custom_call_target="tpu_custom_call" | custom-call | flops 1610612736 | bytes 4194304 | tf_op jit(solution)/shard_map/forward_product/pallas_call | solution.py:270
  114.9 3.1 %forward_product.15 = f32[2,1032,128]{2,1,0:T(8,128)S(1)} custom-call(s32[10]{0:T(128)S(1)} %pad_add_fusion.index_ref, f32[512,128]{1,0:T(8,128)S(1)} %collective-permute-done.10.refs_0_, f32[512,128]{1,0:T(8,128)S(1)} %collective-permute-done.12.refs_1_, bf16[2048,1024]{1,0:T(8,128)(2,1)S(1)} %get-tuple-element.209.refs_2_.refs_3_, ...), custom_call_target="tpu_custom_call" | custom-call | flops 1610612736 | bytes 4194304 | tf_op jit(solution)/shard_map/forward_product/pallas_call | solution.py:270
  118.7 4.0 %collective-permute-done.16 = f32[1032,128]{1,0:T(8,128)S(1)} collective-permute-done((f32[1032,128]{1,0:T(8,128)S(1)}, f32[1032,128]{1,0:T(8,128)S(1)}, u32[]{:S(2)}, u32[]{:S(2)}) %collective-permute-start.16) | collective-permute-done | bytes 528416 | tf_op jit(solution)/shard_map/ppermute | solution.py:325
  124.4 7.6 %collective-permute-done.15 = f32[1032,128]{1,0:T(8,128)S(1)} collective-permute-done((f32[1032,128]{1,0:T(8,128)S(1)}, f32[1032,128]{1,0:T(8,128)S(1)}, u32[]{:S(2)}, u32[]{:S(2)}) %collective-permute-start.15) | collective-permute-done | bytes 528416 | tf_op jit(solution)/shard_map/ppermute | solution.py:325
  135.7 4.1 %adjoint_product.12 = (f32[128,1024]{1,0:T(8,128)S(1)}, f32[128,1024]{1,0:T(8,128)S(1)}, f32[8,128]{1,0:T(8,128)S(1)}) custom-call(s32[10]{0:T(128)S(1)} %pad_add_fusion.index_ref, f32[1024,128]{1,0:T(8,128)S(1)} %slice.158.refs_0_, f32[1024,128]{1,0:T(8,128)S(1)} %collective-permute-done.19.refs_1_, bf16[2048,1024]{1,0:T(8,128)(2,1)S(1)} %get-tuple-element.175.refs_2_, ...), custom_call_target="tpu_custom_call" | custom-call | flops 3221225472 | bytes 8388608 | tf_op jit(solution)/shard_map/adjoint_product/pallas_call | solution.py:203
  145.1 4.0 %collective-permute-done.21.refs_1_ = f32[1024,128]{1,0:T(8,128)S(1)} collective-permute-done((f32[1024,128]{1,0:T(8,128)S(1)}, f32[1024,128]{1,0:T(8,128)S(1)}, u32[]{:S(2)}, u32[]{:S(2)}) %collective-permute-start.21) | collective-permute-done | bytes 524320 | tf_op jit(solution)/shard_map/ppermute | solution.py:325
  149.1 4.1 %adjoint_product.13 = (f32[128,1024]{1,0:T(8,128)S(1)}, f32[128,1024]{1,0:T(8,128)S(1)}, f32[8,128]{1,0:T(8,128)S(1)}) custom-call(s32[10]{0:T(128)S(1)} %pad_add_fusion.index_ref, f32[1024,128]{1,0:T(8,128)S(1)} %collective-permute-done.18.refs_0_, f32[1024,128]{1,0:T(8,128)S(1)} %collective-permute-done.21.refs_1_, bf16[2048,1024]{1,0:T(8,128)(2,1)S(1)} %copy-done.11, ...), custom_call_target="tpu_custom_call" | custom-call | flops 3221225472 | bytes 8388608 | tf_op jit(solution)/shard_map/adjoint_product/pallas_call | solution.py:203
  173.5 10.5 %collective-permute-done.27 = f32[520,128]{1,0:T(8,128)S(1)} collective-permute-done((f32[520,128]{1,0:T(8,128)S(1)}, f32[520,128]{1,0:T(8,128)S(1)}, u32[]{:S(2)}, u32[]{:S(2)}) %collective-permute-start.27) | collective-permute-done | bytes 266272 | tf_op jit(solution)/shard_map/ppermute | solution.py:331
  188.2 8.7 %collective-permute-done.29.refs_1_ = f32[512,128]{1,0:T(8,128)S(1)} collective-permute-done((f32[512,128]{1,0:T(8,128)S(1)}, f32[512,128]{1,0:T(8,128)S(1)}, u32[]{:S(2)}, u32[]{:S(2)}) %collective-permute-start.29) | collective-permute-done | bytes 262176 | tf_op jit(solution)/shard_map/ppermute | solution.py:331
  199.0 5.3 %forward_product.18 = (f32[1024,128]{1,0:T(8,128)S(1)}, f32[1024,128]{1,0:T(8,128)S(1)}, f32[1024,128]{1,0:T(8,128)S(1)}, f32[1024,128]{1,0:T(8,128)S(1)}, f32[8,128]{1,0:T(8,128)S(1)}) custom-call(s32[10]{0:T(128)S(1)} %pad_add_fusion.index_ref, f32[512,128]{1,0:T(8,128)S(1)} %fusion.19.refs_0_, f32[512,128]{1,0:T(8,128)S(1)} %collective-permute-done.29.refs_1_, ...), custom_call_target="tpu_custom_call" | custom-call | flops 3221225472 | bytes 8388608 | tf_op jit(solution)/shard_map/forward_product/pallas_call | solution.py:270
  204.5 5.8 %forward_product.19 = (f32[1024,128]{1,0:T(8,128)S(1)}, f32[1024,128]{1,0:T(8,128)S(1)}, f32[1024,128]{1,0:T(8,128)S(1)}, f32[1024,128]{1,0:T(8,128)S(1)}, f32[8,128]{1,0:T(8,128)}) custom-call(s32[10]{0:T(128)S(1)} %pad_add_fusion.index_ref, f32[512,128]{1,0:T(8,128)S(1)} %fusion.19.refs_0_, f32[512,128]{1,0:T(8,128)S(1)} %collective-permute-done.29.refs_1_, ...), custom_call_target="tpu_custom_call" | custom-call | flops 3221225472 | bytes 8388608 | tf_op jit(solution)/shard_map/forward_product/pallas_call | solution.py:270
  210.8 3.3 %forward_product.23 = f32[2,1032,128]{2,1,0:T(8,128)S(1)} custom-call(s32[10]{0:T(128)S(1)} %pad_add_fusion.index_ref, f32[512,128]{1,0:T(8,128)S(1)} %collective-permute-done.28.refs_0_, f32[512,128]{1,0:T(8,128)S(1)} %collective-permute-done.30.refs_1_, bf16[2048,1024]{1,0:T(8,128)(2,1)S(1)} %get-tuple-element.213.refs_3_.refs_2_, ...), custom_call_target="tpu_custom_call" | custom-call | flops 1610612736 | bytes 4194304 | tf_op jit(solution)/shard_map/forward_product/pallas_call | solution.py:270
  214.3 3.1 %forward_product.20 = f32[2,1032,128]{2,1,0:T(8,128)S(1)} custom-call(s32[10]{0:T(128)S(1)} %pad_add_fusion.index_ref, f32[512,128]{1,0:T(8,128)S(1)} %collective-permute-done.28.refs_0_, f32[512,128]{1,0:T(8,128)S(1)} %collective-permute-done.30.refs_1_, bf16[2048,1024]{1,0:T(8,128)(2,1)S(1)} %get-tuple-element.200.refs_2_.refs_3_, ...), custom_call_target="tpu_custom_call" | custom-call | flops 1610612736 | bytes 4194304 | tf_op jit(solution)/shard_map/forward_product/pallas_call | solution.py:270
  217.4 3.1 %forward_product.22 = f32[2,1032,128]{2,1,0:T(8,128)S(1)} custom-call(s32[10]{0:T(128)S(1)} %pad_add_fusion.index_ref, f32[512,128]{1,0:T(8,128)S(1)} %collective-permute-done.28.refs_0_, f32[512,128]{1,0:T(8,128)S(1)} %collective-permute-done.30.refs_1_, bf16[2048,1024]{1,0:T(8,128)(2,1)S(1)} %get-tuple-element.209.refs_2_.refs_3_, ...), custom_call_target="tpu_custom_call" | custom-call | flops 1610612736 | bytes 4194304 | tf_op jit(solution)/shard_map/forward_product/pallas_call | solution.py:270
  222.7 3.1 %forward_product.21 = f32[2,1032,128]{2,1,0:T(8,128)S(1)} custom-call(s32[10]{0:T(128)S(1)} %pad_add_fusion.index_ref, f32[512,128]{1,0:T(8,128)S(1)} %collective-permute-done.28.refs_0_, f32[512,128]{1,0:T(8,128)S(1)} %collective-permute-done.30.refs_1_, bf16[2048,1024]{1,0:T(8,128)(2,1)S(1)} %get-tuple-element.209.refs_2_.refs_3_, ...), custom_call_target="tpu_custom_call" | custom-call | flops 1610612736 | bytes 4194304 | tf_op jit(solution)/shard_map/forward_product/pallas_call | solution.py:270
  226.4 4.0 %collective-permute-done.34 = f32[1032,128]{1,0:T(8,128)S(1)} collective-permute-done((f32[1032,128]{1,0:T(8,128)S(1)}, f32[1032,128]{1,0:T(8,128)S(1)}, u32[]{:S(2)}, u32[]{:S(2)}) %collective-permute-start.34) | collective-permute-done | bytes 528416 | tf_op jit(solution)/shard_map/ppermute | solution.py:325
  232.1 7.6 %collective-permute-done.33 = f32[1032,128]{1,0:T(8,128)S(1)} collective-permute-done((f32[1032,128]{1,0:T(8,128)S(1)}, f32[1032,128]{1,0:T(8,128)S(1)}, u32[]{:S(2)}, u32[]{:S(2)}) %collective-permute-start.33) | collective-permute-done | bytes 528416 | tf_op jit(solution)/shard_map/ppermute | solution.py:325
  243.5 4.1 %adjoint_product.18 = (f32[128,1024]{1,0:T(8,128)S(1)}, f32[128,1024]{1,0:T(8,128)S(1)}, f32[8,128]{1,0:T(8,128)S(1)}) custom-call(s32[10]{0:T(128)S(1)} %pad_add_fusion.index_ref, f32[1024,128]{1,0:T(8,128)S(1)} %slice_add_fusion.8.refs_0_, f32[1024,128]{1,0:T(8,128)S(1)} %collective-permute-done.37.refs_1_, ...), custom_call_target="tpu_custom_call" | custom-call | flops 3221225472 | bytes 8388608 | tf_op jit(solution)/shard_map/adjoint_product/pallas_call | solution.py:203
  253.0 3.9 %collective-permute-done.39.refs_1_ = f32[1024,128]{1,0:T(8,128)S(1)} collective-permute-done((f32[1024,128]{1,0:T(8,128)S(1)}, f32[1024,128]{1,0:T(8,128)S(1)}, u32[]{:S(2)}, u32[]{:S(2)}) %collective-permute-start.39) | collective-permute-done | bytes 524320 | tf_op jit(solution)/shard_map/ppermute | solution.py:325
  256.9 4.4 %adjoint_product.19 = (f32[128,1024]{1,0:T(8,128)S(1)}, f32[128,1024]{1,0:T(8,128)S(1)}, f32[8,128]{1,0:T(8,128)S(1)}) custom-call(s32[10]{0:T(128)S(1)} %pad_add_fusion.index_ref, f32[1024,128]{1,0:T(8,128)S(1)} %collective-permute-done.36.refs_0_, f32[1024,128]{1,0:T(8,128)S(1)} %collective-permute-done.39.refs_1_, bf16[2048,1024]{1,0:T(8,128)(2,1)S(1)} %copy-done.13, ...), custom_call_target="tpu_custom_call" | custom-call | flops 3221225472 | bytes 8388608 | tf_op jit(solution)/shard_map/adjoint_product/pallas_call | solution.py:203
  280.9 10.5 %collective-permute-done.45 = f32[520,128]{1,0:T(8,128)S(1)} collective-permute-done((f32[520,128]{1,0:T(8,128)S(1)}, f32[520,128]{1,0:T(8,128)S(1)}, u32[]{:S(2)}, u32[]{:S(2)}) %collective-permute-start.45) | collective-permute-done | bytes 266272 | tf_op jit(solution)/shard_map/ppermute | solution.py:331
  (182 shorter events, 94.1 us)
Async XLA Ops:
  1.1 16.8 %collective-permute-start = (f32[1024,128]{1,0:T(8,128)}, f32[1024,128]{1,0:T(8,128)}, u32[]{:S(2)}, u32[]{:S(2)}) collective-permute-start(f32[1024,128]{1,0:T(8,128)} %refs_0_.1), channel_id=1, source_target_pairs={{0,4},{1,3},{2,6},{3,1},{4,0},{5,7},{6,2},{7,5},{8,12},{9,11},{10,... | collective-permute-start | bytes 1572872 | tf_op jit(solution)/shard_map/ppermute | solution.py:325
  3.7 14.8 %collective-permute-start.3 = (f32[1024,128]{1,0:T(8,128)}, f32[1024,128]{1,0:T(8,128)}, u32[]{:S(2)}, u32[]{:S(2)}) collective-permute-start(f32[1024,128]{1,0:T(8,128)} %refs_0_.1), channel_id=1, source_target_pairs={{0,2},{1,5},{2,0},{3,7},{4,6},{5,1},{6,4},{7,3},{8,10},{9,13},{10,... | collective-permute-start | bytes 1572872 | tf_op jit(solution)/shard_map/ppermute | solution.py:325
  18.0 12.3 %collective-permute-start.2 = (f32[1024,128]{1,0:T(8,128)}, f32[1024,128]{1,0:T(8,128)S(1)}, u32[]{:S(2)}, u32[]{:S(2)}) collective-permute-start(f32[1024,128]{1,0:T(8,128)} %collective-permute-done.refs_0_), channel_id=1, source_target_pairs={{0,2},{1,5},{2,0},{3,7},{4,6},{5,1},{6,4},{7,3},{8,10},{9,13},{10,... | collective-permute-start | bytes 1572872 | tf_op jit(solution)/shard_map/ppermute | solution.py:325
  18.5 11.8 %collective-permute-start.5 = (f32[1024,128]{1,0:T(8,128)}, f32[1024,128]{1,0:T(8,128)S(1)}, u32[]{:S(2)}, u32[]{:S(2)}) collective-permute-start(f32[1024,128]{1,0:T(8,128)} %collective-permute-done.refs_0_), channel_id=1, source_target_pairs={{0,1},{1,0},{2,3},{3,2},{4,5},{5,4},{6,7},{7,6},{8,9},{9,8},{10,11... | collective-permute-start | bytes 1572872 | tf_op jit(solution)/shard_map/ppermute | solution.py:328
  18.5 11.8 %collective-permute-start.6 = (f32[1024,128]{1,0:T(8,128)}, f32[1024,128]{1,0:T(8,128)S(1)}, u32[]{:S(2)}, u32[]{:S(2)}) collective-permute-start(f32[1024,128]{1,0:T(8,128)} %collective-permute-done.3.refs_1_), channel_id=1, source_target_pairs={{0,1},{1,0},{2,3},{3,2},{4,5},{5,4},{6,7},{7,6},{8,9},{9,8},{10,11... | collective-permute-start | bytes 1572872 | tf_op jit(solution)/shard_map/ppermute | solution.py:328
  30.2 11.8 %collective-permute-start.4 = (f32[1024,128]{1,0:T(8,128)S(1)}, f32[1024,128]{1,0:T(8,128)S(1)}, u32[]{:S(2)}, u32[]{:S(2)}) collective-permute-start(f32[1024,128]{1,0:T(8,128)S(1)} %collective-permute-done.2.refs_0_), channel_id=1, source_target_pairs={{0,1},{1,0},{2,3},{3,2},{4,5},{5,4},{6,7},{7,6},{8,9},{9,8},{10,11... | collective-permute-start | bytes 1572872 | tf_op jit(solution)/shard_map/ppermute | solution.py:328
  64.3 14.2 %collective-permute-start.9 = (f32[520,128]{1,0:T(8,128)S(1)}, f32[520,128]{1,0:T(8,128)S(1)}, u32[]{:S(2)}, u32[]{:S(2)}) collective-permute-start(f32[520,128]{1,0:T(8,128)S(1)} %bitcast_add_fusion.2), channel_id=1, source_target_pairs={{0,16},{8,24},{16,0},{24,8},{1,17},{9,25},{17,1},{25,9},{2,18},{10... | collective-permute-start | bytes 798728 | tf_op jit(solution)/shard_map/ppermute | solution.py:331
  67.0 11.7 %collective-permute-start.8 = (f32[520,128]{1,0:T(8,128)S(1)}, f32[520,128]{1,0:T(8,128)S(1)}, u32[]{:S(2)}, u32[]{:S(2)}) collective-permute-start(f32[520,128]{1,0:T(8,128)S(1)} %get-tuple-element.173), channel_id=1, source_target_pairs={{0,8},{8,0},{16,24},{24,16},{1,9},{9,1},{17,25},{25,17},{2,10},{10... | collective-permute-start | bytes 798728 | tf_op jit(solution)/shard_map/ppermute | solution.py:331
  78.7 12.4 %collective-permute-start.11 = (f32[512,128]{1,0:T(8,128)S(1)}, f32[512,128]{1,0:T(8,128)S(1)}, u32[]{:S(2)}, u32[]{:S(2)}) collective-permute-start(f32[512,128]{1,0:T(8,128)S(1)} %slice_add_fusion.9.refs_0_), channel_id=1, source_target_pairs={{0,8},{8,0},{16,24},{24,16},{1,9},{9,1},{17,25},{25,17},{2,10},{10... | collective-permute-start | bytes 786440 | tf_op jit(solution)/shard_map/ppermute | solution.py:331
  80.2 16.2 %collective-permute-start.10 = (f32[512,128]{1,0:T(8,128)S(1)}, f32[512,128]{1,0:T(8,128)S(1)}, u32[]{:S(2)}, u32[]{:S(2)}) collective-permute-start(f32[512,128]{1,0:T(8,128)S(1)} %slice_add_fusion.9.refs_0_), channel_id=1, source_target_pairs={{0,16},{8,24},{16,0},{24,8},{1,17},{9,25},{17,1},{25,9},{2,18},{10... | collective-permute-start | bytes 786440 | tf_op jit(solution)/shard_map/ppermute | solution.py:331
  113.4 9.3 %collective-permute-start.16 = (f32[1032,128]{1,0:T(8,128)S(1)}, f32[1032,128]{1,0:T(8,128)S(1)}, u32[]{:S(2)}, u32[]{:S(2)}) collective-permute-start(f32[1032,128]{1,0:T(8,128)S(1)} %get-tuple-element.302), channel_id=1, source_target_pairs={{0,2},{1,5},{2,0},{3,7},{4,6},{5,1},{6,4},{7,3},{8,10},{9,13},{10,... | collective-permute-start | bytes 1585160 | tf_op jit(solution)/shard_map/ppermute | solution.py:325
  118.0 14.0 %collective-permute-start.15 = (f32[1032,128]{1,0:T(8,128)S(1)}, f32[1032,128]{1,0:T(8,128)S(1)}, u32[]{:S(2)}, u32[]{:S(2)}) collective-permute-start(f32[1032,128]{1,0:T(8,128)S(1)} %get-tuple-element.301), channel_id=1, source_target_pairs={{0,2},{1,5},{2,0},{3,7},{4,6},{5,1},{6,4},{7,3},{8,10},{9,13},{10,... | collective-permute-start | bytes 1585160 | tf_op jit(solution)/shard_map/ppermute | solution.py:325
  122.8 10.3 %collective-permute-start.17 = (f32[1032,128]{1,0:T(8,128)S(1)}, f32[1032,128]{1,0:T(8,128)S(1)}, u32[]{:S(2)}, u32[]{:S(2)}) collective-permute-start(f32[1032,128]{1,0:T(8,128)S(1)} %fusion.9), channel_id=1, source_target_pairs={{0,4},{1,3},{2,6},{3,1},{4,0},{5,7},{6,2},{7,5},{8,12},{9,11},{10,... | collective-permute-start | bytes 1585160 | tf_op jit(solution)/shard_map/ppermute | solution.py:325
  134.1 9.5 %collective-permute-start.18 = (f32[1024,128]{1,0:T(8,128)S(1)}, f32[1024,128]{1,0:T(8,128)S(1)}, u32[]{:S(2)}, u32[]{:S(2)}) collective-permute-start(f32[1024,128]{1,0:T(8,128)S(1)} %slice.158.refs_0_), channel_id=1, source_target_pairs={{0,4},{1,3},{2,6},{3,1},{4,0},{5,7},{6,2},{7,5},{8,12},{9,11},{10,... | collective-permute-start | bytes 1572872 | tf_op jit(solution)/shard_map/ppermute | solution.py:325
  139.9 9.2 %collective-permute-start.21 = (f32[1024,128]{1,0:T(8,128)S(1)}, f32[1024,128]{1,0:T(8,128)S(1)}, u32[]{:S(2)}, u32[]{:S(2)}) collective-permute-start(f32[1024,128]{1,0:T(8,128)S(1)} %slice.158.refs_0_), channel_id=1, source_target_pairs={{0,2},{1,5},{2,0},{3,7},{4,6},{5,1},{6,4},{7,3},{8,10},{9,13},{10,... | collective-permute-start | bytes 1572872 | tf_op jit(solution)/shard_map/ppermute | solution.py:325
  143.6 11.1 %collective-permute-start.20 = (f32[1024,128]{1,0:T(8,128)S(1)}, f32[1024,128]{1,0:T(8,128)S(1)}, u32[]{:S(2)}, u32[]{:S(2)}) collective-permute-start(f32[1024,128]{1,0:T(8,128)S(1)} %collective-permute-done.18.refs_0_), channel_id=1, source_target_pairs={{0,2},{1,5},{2,0},{3,7},{4,6},{5,1},{6,4},{7,3},{8,10},{9,13},{10,... | collective-permute-start | bytes 1572872 | tf_op jit(solution)/shard_map/ppermute | solution.py:325
  145.1 9.7 %collective-permute-start.23 = (f32[1024,128]{1,0:T(8,128)S(1)}, f32[1024,128]{1,0:T(8,128)S(1)}, u32[]{:S(2)}, u32[]{:S(2)}) collective-permute-start(f32[1024,128]{1,0:T(8,128)S(1)} %collective-permute-done.18.refs_0_), channel_id=1, source_target_pairs={{0,1},{1,0},{2,3},{3,2},{4,5},{5,4},{6,7},{7,6},{8,9},{9,8},{10,11... | collective-permute-start | bytes 1572872 | tf_op jit(solution)/shard_map/ppermute | solution.py:328
  160.1 8.9 %collective-permute-start.25 = (f32[520,128]{1,0:T(8,128)S(1)}, f32[520,128]{1,0:T(8,128)S(1)}, u32[]{:S(2)}, u32[]{:S(2)}) collective-permute-start(f32[520,128]{1,0:T(8,128)S(1)} %slice_bitcast_fusion.5), channel_id=1, source_target_pairs={{0,8},{8,0},{16,24},{24,16},{1,9},{9,1},{17,25},{25,17},{2,10},{10... | collective-permute-start | bytes 798728 | tf_op jit(solution)/shard_map/ppermute | solution.py:331
  169.0 15.0 %collective-permute-start.27 = (f32[520,128]{1,0:T(8,128)S(1)}, f32[520,128]{1,0:T(8,128)S(1)}, u32[]{:S(2)}, u32[]{:S(2)}) collective-permute-start(f32[520,128]{1,0:T(8,128)S(1)} %bitcast_add_fusion.1), channel_id=1, source_target_pairs={{0,16},{8,24},{16,0},{24,8},{1,17},{9,25},{17,1},{25,9},{2,18},{10... | collective-permute-start | bytes 798728 | tf_op jit(solution)/shard_map/ppermute | solution.py:331
  171.9 12.3 %collective-permute-start.26 = (f32[520,128]{1,0:T(8,128)S(1)}, f32[520,128]{1,0:T(8,128)S(1)}, u32[]{:S(2)}, u32[]{:S(2)}) collective-permute-start(f32[520,128]{1,0:T(8,128)S(1)} %slice_bitcast_fusion.2), channel_id=1, source_target_pairs={{0,8},{8,0},{16,24},{24,16},{1,9},{9,1},{17,25},{25,17},{2,10},{10... | collective-permute-start | bytes 798728 | tf_op jit(solution)/shard_map/ppermute | solution.py:331
  184.4 12.5 %collective-permute-start.29 = (f32[512,128]{1,0:T(8,128)S(1)}, f32[512,128]{1,0:T(8,128)S(1)}, u32[]{:S(2)}, u32[]{:S(2)}) collective-permute-start(f32[512,128]{1,0:T(8,128)S(1)} %fusion.19.refs_0_), channel_id=1, source_target_pairs={{0,8},{8,0},{16,24},{24,16},{1,9},{9,1},{17,25},{25,17},{2,10},{10... | collective-permute-start | bytes 786440 | tf_op jit(solution)/shard_map/ppermute | solution.py:331
  185.9 18.5 %collective-permute-start.28 = (f32[512,128]{1,0:T(8,128)S(1)}, f32[512,128]{1,0:T(8,128)S(1)}, u32[]{:S(2)}, u32[]{:S(2)}) collective-permute-start(f32[512,128]{1,0:T(8,128)S(1)} %fusion.19.refs_0_), channel_id=1, source_target_pairs={{0,16},{8,24},{16,0},{24,8},{1,17},{9,25},{17,1},{25,9},{2,18},{10... | collective-permute-start | bytes 786440 | tf_op jit(solution)/shard_map/ppermute | solution.py:331
  221.2 9.3 %collective-permute-start.34 = (f32[1032,128]{1,0:T(8,128)S(1)}, f32[1032,128]{1,0:T(8,128)S(1)}, u32[]{:S(2)}, u32[]{:S(2)}) collective-permute-start(f32[1032,128]{1,0:T(8,128)S(1)} %get-tuple-element.300), channel_id=1, source_target_pairs={{0,2},{1,5},{2,0},{3,7},{4,6},{5,1},{6,4},{7,3},{8,10},{9,13},{10,... | collective-permute-start | bytes 1585160 | tf_op jit(solution)/shard_map/ppermute | solution.py:325
  225.8 14.0 %collective-permute-start.33 = (f32[1032,128]{1,0:T(8,128)S(1)}, f32[1032,128]{1,0:T(8,128)S(1)}, u32[]{:S(2)}, u32[]{:S(2)}) collective-permute-start(f32[1032,128]{1,0:T(8,128)S(1)} %get-tuple-element.299), channel_id=1, source_target_pairs={{0,2},{1,5},{2,0},{3,7},{4,6},{5,1},{6,4},{7,3},{8,10},{9,13},{10,... | collective-permute-start | bytes 1585160 | tf_op jit(solution)/shard_map/ppermute | solution.py:325
  230.6 10.3 %collective-permute-start.35 = (f32[1032,128]{1,0:T(8,128)S(1)}, f32[1032,128]{1,0:T(8,128)S(1)}, u32[]{:S(2)}, u32[]{:S(2)}) collective-permute-start(f32[1032,128]{1,0:T(8,128)S(1)} %fusion.2), channel_id=1, source_target_pairs={{0,4},{1,3},{2,6},{3,1},{4,0},{5,7},{6,2},{7,5},{8,12},{9,11},{10,... | collective-permute-start | bytes 1585160 | tf_op jit(solution)/shard_map/ppermute | solution.py:325
  241.9 9.6 %collective-permute-start.36 = (f32[1024,128]{1,0:T(8,128)S(1)}, f32[1024,128]{1,0:T(8,128)S(1)}, u32[]{:S(2)}, u32[]{:S(2)}) collective-permute-start(f32[1024,128]{1,0:T(8,128)S(1)} %slice_add_fusion.8.refs_0_), channel_id=1, source_target_pairs={{0,4},{1,3},{2,6},{3,1},{4,0},{5,7},{6,2},{7,5},{8,12},{9,11},{10,... | collective-permute-start | bytes 1572872 | tf_op jit(solution)/shard_map/ppermute | solution.py:325
  247.6 9.2 %collective-permute-start.39 = (f32[1024,128]{1,0:T(8,128)S(1)}, f32[1024,128]{1,0:T(8,128)S(1)}, u32[]{:S(2)}, u32[]{:S(2)}) collective-permute-start(f32[1024,128]{1,0:T(8,128)S(1)} %slice_add_fusion.8.refs_0_), channel_id=1, source_target_pairs={{0,2},{1,5},{2,0},{3,7},{4,6},{5,1},{6,4},{7,3},{8,10},{9,13},{10,... | collective-permute-start | bytes 1572872 | tf_op jit(solution)/shard_map/ppermute | solution.py:325
  251.5 10.9 %collective-permute-start.38 = (f32[1024,128]{1,0:T(8,128)S(1)}, f32[1024,128]{1,0:T(8,128)S(1)}, u32[]{:S(2)}, u32[]{:S(2)}) collective-permute-start(f32[1024,128]{1,0:T(8,128)S(1)} %collective-permute-done.36.refs_0_), channel_id=1, source_target_pairs={{0,2},{1,5},{2,0},{3,7},{4,6},{5,1},{6,4},{7,3},{8,10},{9,13},{10,... | collective-permute-start | bytes 1572872 | tf_op jit(solution)/shard_map/ppermute | solution.py:325
  253.0 9.5 %collective-permute-start.41 = (f32[1024,128]{1,0:T(8,128)S(1)}, f32[1024,128]{1,0:T(8,128)S(1)}, u32[]{:S(2)}, u32[]{:S(2)}) collective-permute-start(f32[1024,128]{1,0:T(8,128)S(1)} %collective-permute-done.36.refs_0_), channel_id=1, source_target_pairs={{0,1},{1,0},{2,3},{3,2},{4,5},{5,4},{6,7},{7,6},{8,9},{9,8},{10,11... | collective-permute-start | bytes 1572872 | tf_op jit(solution)/shard_map/ppermute | solution.py:328
  267.6 8.9 %collective-permute-start.43 = (f32[520,128]{1,0:T(8,128)S(1)}, f32[520,128]{1,0:T(8,128)S(1)}, u32[]{:S(2)}, u32[]{:S(2)}) collective-permute-start(f32[520,128]{1,0:T(8,128)S(1)} %slice_bitcast_fusion.4), channel_id=1, source_target_pairs={{0,8},{8,0},{16,24},{24,16},{1,9},{9,1},{17,25},{25,17},{2,10},{10... | collective-permute-start | bytes 798728 | tf_op jit(solution)/shard_map/ppermute | solution.py:331
  276.6 14.9 %collective-permute-start.45 = (f32[520,128]{1,0:T(8,128)S(1)}, f32[520,128]{1,0:T(8,128)S(1)}, u32[]{:S(2)}, u32[]{:S(2)}) collective-permute-start(f32[520,128]{1,0:T(8,128)S(1)} %bitcast_add_fusion), channel_id=1, source_target_pairs={{0,16},{8,24},{16,0},{24,8},{1,17},{9,25},{17,1},{25,9},{2,18},{10... | collective-permute-start | bytes 798728 | tf_op jit(solution)/shard_map/ppermute | solution.py:331
  279.3 12.4 %collective-permute-start.44 = (f32[520,128]{1,0:T(8,128)S(1)}, f32[520,128]{1,0:T(8,128)S(1)}, u32[]{:S(2)}, u32[]{:S(2)}) collective-permute-start(f32[520,128]{1,0:T(8,128)S(1)} %slice_bitcast_fusion), channel_id=1, source_target_pairs={{0,8},{8,0},{16,24},{24,16},{1,9},{9,1},{17,25},{25,17},{2,10},{10... | collective-permute-start | bytes 798728 | tf_op jit(solution)/shard_map/ppermute | solution.py:331
  (46 other events, 619.0 us)
where the time goes:
time: 300 us; the launch traced here: 294 us
  Pallas kernels  133 us (44%)
  waiting for transfers between devices  101 us (34%)
  starting transfers between devices  50.9 us (17%)
  other arithmetic  3.58 us (1%)
  local copies, waits for them, and re-layouts  3.58 us (1%)
    ppermute x15, waiting for transfers between devices, between(): return lax.ppermute(piece, 'pix', pix_perm[b])  60.7 us
    pallas_call x12, Pallas kernels, forward_call(): pl.pallas_call(functools.partial(forward_kernel, len(x_parts), len(used),...  47.7 us
    pallas_call x4, Pallas kernels, first_call(): pl.pallas_call(functools.partial(first_kernel, count, per_chunk, carry is...  47.7 us
    ppermute x15, waiting for transfers between devices, stage(): return lax.ppermute(piece, 'cell', stage_perm[j])  40.6 us
    pallas_call x12, Pallas kernels, adjoint_call(): pl.pallas_call(functools.partial(adjoint_kernel, count, sides, last), in_...  37.2 us
    ppermute x15, starting transfers between devices, between(): return lax.ppermute(piece, 'pix', pix_perm[b])  25.8 us
    ppermute x15, starting transfers between devices, stage(): return lax.ppermute(piece, 'cell', stage_perm[j])  21.1 us
  transfers between devices with their start and end apart: 46, of which 25 were waited for; matrix products, arithmetic and copies ran while one was open for 0% of the time, Pallas kernels for 36%

commit v1 on v0

--- a/solution.py
+++ b/solution.py
@@ -9,7 +9,7 @@
 
 ITERS = 2
 BLOCK_ROWS = 512
-FIRST_LIMIT = 18 * 2**20
+FIRST_LIMIT = 20 * 2**20
 LATER_LIMIT = 9 * 2**20
 f32 = jnp.float32
 bf16 = jnp.bfloat16
@@ -239,12 +239,19 @@
         cat_ref[pl.ds(start, cells), :frames] = high
         cat_ref[pl.ds(start, cells), frames:] = low
         total = total + squares(x)
+    top = x_refs[0][...]
+    top = jnp.max(jnp.abs(top), axis=0, keepdims=True)
+    for part in range(1, parts):
+        top = jnp.maximum(top, jnp.max(jnp.abs(x_refs[part][...]), axis=0, keepdims=True))
+    top = jnp.maximum(top, 1e-30)
+    narrow = (cat_ref[:, :frames].astype(f32) * (224.0 / top)).astype(f8)
+    widen = top * (1.0 / 224.0)
     if near:
         sum_out[...] = jnp.broadcast_to(total, sum_out.shape)
     for i, (which, row) in enumerate(places):
         both = jnp.dot(highs[which][row : row + chunk_rows, :], cat_ref[...], preferred_element_type=f32)
         value = both[:, :frames] + both[:, frames:]
-        other = jnp.dot(lows[which][row : row + chunk_rows, :].astype(bf16), cat_ref[:, :frames], preferred_element_type=f32)
+        other = jnp.dot(lows[which][row : row + chunk_rows, :], narrow, preferred_element_type=f32) * widen
         rows = highs[which].shape[0] // scales[which].shape[0]
         for start in range(0, chunk_rows, rows):
             at = slice(start, start + rows)

time: 300 us -> 293 us (0.977)
  Pallas kernels: 133 us -> 124 us
  waiting for transfers between devices: 101 us -> 105 us
    pallas_call x12, Pallas kernels: 47.7 us -> 39.6 us  [forward_call(): pl.pallas_call(functools.partial(forward_kernel, len(x_parts), len(used),...]
  transfers between devices with their start and end apart: 46 -> 46, of which waited for: 25 -> 27; matrix products, arithmetic and copies ran while one was open for 0% -> 0% of each run, Pallas kernels for 36% -> 35%
where the time goes in v1:
time: 293 us; the launch traced here: 288 us
  Pallas kernels  124 us (42%)
  waiting for transfers between devices  105 us (36%)
  starting transfers between devices  49.6 us (17%)
  other arithmetic  3.64 us (1%)
  local copies, waits for them, and re-layouts  3.55 us (1%)
    ppermute x15, waiting for transfers between devices, between(): return lax.ppermute(piece, 'pix', pix_perm[b])  63.7 us
    pallas_call x4, Pallas kernels, first_call(): pl.pallas_call(functools.partial(first_kernel, count, per_chunk, carry is...  47.5 us
    ppermute x15, waiting for transfers between devices, stage(): return lax.ppermute(piece, 'cell', stage_perm[j])  41.2 us
    pallas_call x12, Pallas kernels, forward_call(): pl.pallas_call(functools.partial(forward_kernel, len(x_parts), len(used),...  39.6 us
    pallas_call x12, Pallas kernels, adjoint_call(): pl.pallas_call(functools.partial(adjoint_kernel, count, sides, last), in_...  36.9 us
    ppermute x15, starting transfers between devices, between(): return lax.ppermute(piece, 'pix', pix_perm[b])  24.2 us
    ppermute x15, starting transfers between devices, stage(): return lax.ppermute(piece, 'cell', stage_perm[j])  21.3 us
  transfers between devices with their start and end apart: 46, of which 27 were waited for; matrix products, arithmetic and copies ran while one was open for 0% of the time, Pallas kernels for 35%

profile of v1, /device:TPU:0, one launch (start us, length us, event | category | flops | bytes accessed | tf_op | source)
XLA Modules:
  0.0 287.6 jit_solution(10870976283540429642)
XLA Ops:
  7.0 11.0 %first_adjoint.4 = (bf16[2048,1024]{1,0:T(8,128)(2,1)S(1)}, bf16[2048,1024]{1,0:T(8,128)(2,1)S(1)}, f8e4m3fn[2048,1024]{1,0:T(32,128)(4,1)}, f8e4m3fn[2048,1024]...) custom-call(s32[10]{0:T(128)S(1)} %pad_add_fusion.index_ref, ...), custom_call_target="tpu_custom_call" | custom-call | flops 3221225472 | bytes 16777216 | tf_op jit(solution)/shard_map/first_adjoint/pallas_call | solution.py:131
  19.1 10.9 %first_adjoint.5 = (bf16[2048,1024]{1,0:T(8,128)(2,1)S(1)}, bf16[2048,1024]{1,0:T(8,128)(2,1)S(1)}, f8e4m3fn[2048,1024]{1,0:T(32,128)(4,1)}, f8e4m3fn[2048,1024]...) custom-call(s32[10]{0:T(128)S(1)} %pad_add_fusion.index_ref, ...), custom_call_target="tpu_custom_call" | custom-call | flops 3221225472 | bytes 16777216 | tf_op jit(solution)/shard_map/first_adjoint/pallas_call | solution.py:131
  30.1 11.8 %first_adjoint.6 = (bf16[2048,1024]{1,0:T(8,128)(2,1)S(1)}, bf16[2048,1024]{1,0:T(8,128)(2,1)S(1)}, f8e4m3fn[2048,1024]{1,0:T(32,128)(4,1)}, f8e4m3fn[2048,1024]...) custom-call(s32[10]{0:T(128)S(1)} %pad_add_fusion.index_ref, ...), custom_call_target="tpu_custom_call" | custom-call | flops 3221225472 | bytes 16777216 | tf_op jit(solution)/shard_map/first_adjoint/pallas_call | solution.py:131
  41.9 13.8 %first_adjoint.7 = (bf16[2048,1024]{1,0:T(8,128)(2,1)S(1)}, bf16[2048,1024]{1,0:T(8,128)(2,1)S(1)}, f8e4m3fn[2048,1024]{1,0:T(32,128)(4,1)}, f8e4m3fn[2048,1024]...) custom-call(s32[10]{0:T(128)S(1)} %pad_add_fusion.index_ref, ...), custom_call_target="tpu_custom_call" | custom-call | flops 3221225472 | bytes 16777216 | tf_op jit(solution)/shard_map/first_adjoint/pallas_call | solution.py:131
  57.5 6.6 %collective-permute-done.7 = f32[520,128]{1,0:T(8,128)S(1)} collective-permute-done((f32[520,128]{1,0:T(8,128)S(1)}, f32[520,128]{1,0:T(8,128)S(1)}, u32[]{:S(2)}, u32[]{:S(2)}) %collective-permute-start.7) | collective-permute-done | bytes 266272 | tf_op jit(solution)/shard_map/ppermute | solution.py:338
  64.1 2.6 collective-permute-start.9
  68.4 9.9 %collective-permute-done.9 = f32[520,128]{1,0:T(8,128)S(1)} collective-permute-done((f32[520,128]{1,0:T(8,128)S(1)}, f32[520,128]{1,0:T(8,128)S(1)}, u32[]{:S(2)}, u32[]{:S(2)}) %collective-permute-start.9) | collective-permute-done | bytes 266272 | tf_op jit(solution)/shard_map/ppermute | solution.py:338
  82.3 8.5 %collective-permute-done.11.refs_1_ = f32[512,128]{1,0:T(8,128)S(1)} collective-permute-done((f32[512,128]{1,0:T(8,128)S(1)}, f32[512,128]{1,0:T(8,128)S(1)}, u32[]{:S(2)}, u32[]{:S(2)}) %collective-permute-start.11) | collective-permute-done | bytes 262176 | tf_op jit(solution)/shard_map/ppermute | solution.py:338
  90.8 4.3 %forward_product.12 = (f32[1024,128]{1,0:T(8,128)S(1)}, f32[1024,128]{1,0:T(8,128)S(1)}, f32[1024,128]{1,0:T(8,128)S(1)}, f32[1024,128]{1,0:T(8,128)S(1)}, f32[8,128]{1,0:T(8,128)S(1)}) custom-call(s32[10]{0:T(128)S(1)} %pad_add_fusion.index_ref, f32[512,128]{1,0:T(8,128)S(1)} %slice_add_fusion.9.refs_0_, f32[512,128]{1,0:T(8,128)S(1)} %collective-permute-done.11.refs_1_, ...), custom_call_target="tpu_custom_call" | custom-call | flops 3221225472 | bytes 8388608 | tf_op jit(solution)/shard_map/forward_product/pallas_call | solution.py:277
  95.2 4.8 %forward_product.13 = (f32[1024,128]{1,0:T(8,128)S(1)}, f32[1024,128]{1,0:T(8,128)S(1)}, f32[1024,128]{1,0:T(8,128)S(1)}, f32[1024,128]{1,0:T(8,128)S(1)}, f32[8,128]{1,0:T(8,128)}) custom-call(s32[10]{0:T(128)S(1)} %pad_add_fusion.index_ref, f32[512,128]{1,0:T(8,128)S(1)} %slice_add_fusion.9.refs_0_, f32[512,128]{1,0:T(8,128)S(1)} %collective-permute-done.11.refs_1_, ...), custom_call_target="tpu_custom_call" | custom-call | flops 3221225472 | bytes 8388608 | tf_op jit(solution)/shard_map/forward_product/pallas_call | solution.py:277
  111.8 3.0 %forward_product.15 = f32[2,1032,128]{2,1,0:T(8,128)S(1)} custom-call(s32[10]{0:T(128)S(1)} %pad_add_fusion.index_ref, f32[512,128]{1,0:T(8,128)S(1)} %collective-permute-done.10.refs_0_, f32[512,128]{1,0:T(8,128)S(1)} %collective-permute-done.12.refs_1_, bf16[2048,1024]{1,0:T(8,128)(2,1)S(1)} %get-tuple-element.209.refs_2_.refs_3_, ...), custom_call_target="tpu_custom_call" | custom-call | flops 1610612736 | bytes 4194304 | tf_op jit(solution)/shard_map/forward_product/pallas_call | solution.py:277
  115.3 4.1 %collective-permute-done.16 = f32[1032,128]{1,0:T(8,128)S(1)} collective-permute-done((f32[1032,128]{1,0:T(8,128)S(1)}, f32[1032,128]{1,0:T(8,128)S(1)}, u32[]{:S(2)}, u32[]{:S(2)}) %collective-permute-start.16) | collective-permute-done | bytes 528416 | tf_op jit(solution)/shard_map/ppermute | solution.py:332
  121.1 7.7 %collective-permute-done.15 = f32[1032,128]{1,0:T(8,128)S(1)} collective-permute-done((f32[1032,128]{1,0:T(8,128)S(1)}, f32[1032,128]{1,0:T(8,128)S(1)}, u32[]{:S(2)}, u32[]{:S(2)}) %collective-permute-start.15) | collective-permute-done | bytes 528416 | tf_op jit(solution)/shard_map/ppermute | solution.py:332
  132.5 4.1 %adjoint_product.12 = (f32[128,1024]{1,0:T(8,128)S(1)}, f32[128,1024]{1,0:T(8,128)S(1)}, f32[8,128]{1,0:T(8,128)S(1)}) custom-call(s32[10]{0:T(128)S(1)} %pad_add_fusion.index_ref, f32[1024,128]{1,0:T(8,128)S(1)} %slice.158.refs_0_, f32[1024,128]{1,0:T(8,128)S(1)} %collective-permute-done.19.refs_1_, bf16[2048,1024]{1,0:T(8,128)(2,1)S(1)} %get-tuple-element.175.refs_2_, ...), custom_call_target="tpu_custom_call" | custom-call | flops 3221225472 | bytes 8388608 | tf_op jit(solution)/shard_map/adjoint_product/pallas_call | solution.py:203
  142.0 3.8 %collective-permute-done.21.refs_1_ = f32[1024,128]{1,0:T(8,128)S(1)} collective-permute-done((f32[1024,128]{1,0:T(8,128)S(1)}, f32[1024,128]{1,0:T(8,128)S(1)}, u32[]{:S(2)}, u32[]{:S(2)}) %collective-permute-start.21) | collective-permute-done | bytes 524320 | tf_op jit(solution)/shard_map/ppermute | solution.py:332
  145.8 4.1 %adjoint_product.13 = (f32[128,1024]{1,0:T(8,128)S(1)}, f32[128,1024]{1,0:T(8,128)S(1)}, f32[8,128]{1,0:T(8,128)S(1)}) custom-call(s32[10]{0:T(128)S(1)} %pad_add_fusion.index_ref, f32[1024,128]{1,0:T(8,128)S(1)} %collective-permute-done.18.refs_0_, f32[1024,128]{1,0:T(8,128)S(1)} %collective-permute-done.21.refs_1_, bf16[2048,1024]{1,0:T(8,128)(2,1)S(1)} %copy-done.13, ...), custom_call_target="tpu_custom_call" | custom-call | flops 3221225472 | bytes 8388608 | tf_op jit(solution)/shard_map/adjoint_product/pallas_call | solution.py:203
  162.5 2.9 %collective-permute-done.25 = f32[520,128]{1,0:T(8,128)S(1)} collective-permute-done((f32[520,128]{1,0:T(8,128)S(1)}, f32[520,128]{1,0:T(8,128)S(1)}, u32[]{:S(2)}, u32[]{:S(2)}) %collective-permute-start.25) | collective-permute-done | bytes 266272 | tf_op jit(solution)/shard_map/ppermute | solution.py:338
  165.5 2.8 collective-permute-start.27
  170.0 10.4 %collective-permute-done.27 = f32[520,128]{1,0:T(8,128)S(1)} collective-permute-done((f32[520,128]{1,0:T(8,128)S(1)}, f32[520,128]{1,0:T(8,128)S(1)}, u32[]{:S(2)}, u32[]{:S(2)}) %collective-permute-start.27) | collective-permute-done | bytes 266272 | tf_op jit(solution)/shard_map/ppermute | solution.py:338
  184.6 8.5 %collective-permute-done.29.refs_1_ = f32[512,128]{1,0:T(8,128)S(1)} collective-permute-done((f32[512,128]{1,0:T(8,128)S(1)}, f32[512,128]{1,0:T(8,128)S(1)}, u32[]{:S(2)}, u32[]{:S(2)}) %collective-permute-start.29) | collective-permute-done | bytes 262176 | tf_op jit(solution)/shard_map/ppermute | solution.py:338
  195.3 4.3 %forward_product.18 = (f32[1024,128]{1,0:T(8,128)S(1)}, f32[1024,128]{1,0:T(8,128)S(1)}, f32[1024,128]{1,0:T(8,128)S(1)}, f32[1024,128]{1,0:T(8,128)S(1)}, f32[8,128]{1,0:T(8,128)S(1)}) custom-call(s32[10]{0:T(128)S(1)} %pad_add_fusion.index_ref, f32[512,128]{1,0:T(8,128)S(1)} %fusion.19.refs_0_, f32[512,128]{1,0:T(8,128)S(1)} %collective-permute-done.29.refs_1_, ...), custom_call_target="tpu_custom_call" | custom-call | flops 3221225472 | bytes 8388608 | tf_op jit(solution)/shard_map/forward_product/pallas_call | solution.py:277
  199.7 4.8 %forward_product.19 = (f32[1024,128]{1,0:T(8,128)S(1)}, f32[1024,128]{1,0:T(8,128)S(1)}, f32[1024,128]{1,0:T(8,128)S(1)}, f32[1024,128]{1,0:T(8,128)S(1)}, f32[8,128]{1,0:T(8,128)}) custom-call(s32[10]{0:T(128)S(1)} %pad_add_fusion.index_ref, f32[512,128]{1,0:T(8,128)S(1)} %fusion.19.refs_0_, f32[512,128]{1,0:T(8,128)S(1)} %collective-permute-done.29.refs_1_, ...), custom_call_target="tpu_custom_call" | custom-call | flops 3221225472 | bytes 8388608 | tf_op jit(solution)/shard_map/forward_product/pallas_call | solution.py:277
  208.7 2.8 forward_product.20
  219.6 4.5 %collective-permute-done.34 = f32[1032,128]{1,0:T(8,128)S(1)} collective-permute-done((f32[1032,128]{1,0:T(8,128)S(1)}, f32[1032,128]{1,0:T(8,128)S(1)}, u32[]{:S(2)}, u32[]{:S(2)}) %collective-permute-start.34) | collective-permute-done | bytes 528416 | tf_op jit(solution)/shard_map/ppermute | solution.py:332
  225.7 7.7 %collective-permute-done.33 = f32[1032,128]{1,0:T(8,128)S(1)} collective-permute-done((f32[1032,128]{1,0:T(8,128)S(1)}, f32[1032,128]{1,0:T(8,128)S(1)}, u32[]{:S(2)}, u32[]{:S(2)}) %collective-permute-start.33) | collective-permute-done | bytes 528416 | tf_op jit(solution)/shard_map/ppermute | solution.py:332
  237.1 4.1 %adjoint_product.18 = (f32[128,1024]{1,0:T(8,128)S(1)}, f32[128,1024]{1,0:T(8,128)S(1)}, f32[8,128]{1,0:T(8,128)S(1)}) custom-call(s32[10]{0:T(128)S(1)} %pad_add_fusion.index_ref, f32[1024,128]{1,0:T(8,128)S(1)} %slice_add_fusion.8.refs_0_, f32[1024,128]{1,0:T(8,128)S(1)} %collective-permute-done.37.refs_1_, ...), custom_call_target="tpu_custom_call" | custom-call | flops 3221225472 | bytes 8388608 | tf_op jit(solution)/shard_map/adjoint_product/pallas_call | solution.py:203
  246.8 3.7 %collective-permute-done.39.refs_1_ = f32[1024,128]{1,0:T(8,128)S(1)} collective-permute-done((f32[1024,128]{1,0:T(8,128)S(1)}, f32[1024,128]{1,0:T(8,128)S(1)}, u32[]{:S(2)}, u32[]{:S(2)}) %collective-permute-start.39) | collective-permute-done | bytes 524320 | tf_op jit(solution)/shard_map/ppermute | solution.py:332
  250.5 4.1 %adjoint_product.19 = (f32[128,1024]{1,0:T(8,128)S(1)}, f32[128,1024]{1,0:T(8,128)S(1)}, f32[8,128]{1,0:T(8,128)S(1)}) custom-call(s32[10]{0:T(128)S(1)} %pad_add_fusion.index_ref, f32[1024,128]{1,0:T(8,128)S(1)} %collective-permute-done.36.refs_0_, f32[1024,128]{1,0:T(8,128)S(1)} %collective-permute-done.39.refs_1_, bf16[2048,1024]{1,0:T(8,128)(2,1)S(1)} %copy-done.15, ...), custom_call_target="tpu_custom_call" | custom-call | flops 3221225472 | bytes 8388608 | tf_op jit(solution)/shard_map/adjoint_product/pallas_call | solution.py:203
  256.1 2.7 adjoint_product.20
  267.1 3.2 %collective-permute-done.43 = f32[520,128]{1,0:T(8,128)S(1)} collective-permute-done((f32[520,128]{1,0:T(8,128)S(1)}, f32[520,128]{1,0:T(8,128)S(1)}, u32[]{:S(2)}, u32[]{:S(2)}) %collective-permute-start.43) | collective-permute-done | bytes 266272 | tf_op jit(solution)/shard_map/ppermute | solution.py:338
  270.4 2.7 collective-permute-start.45
  274.8 10.3 %collective-permute-done.45 = f32[520,128]{1,0:T(8,128)S(1)} collective-permute-done((f32[520,128]{1,0:T(8,128)S(1)}, f32[520,128]{1,0:T(8,128)S(1)}, u32[]{:S(2)}, u32[]{:S(2)}) %collective-permute-start.45) | collective-permute-done | bytes 266272 | tf_op jit(solution)/shard_map/ppermute | solution.py:338
  (172 shorter events, 95.4 us)
Async XLA Ops:
  1.1 16.8 %collective-permute-start = (f32[1024,128]{1,0:T(8,128)}, f32[1024,128]{1,0:T(8,128)S(1)}, u32[]{:S(2)}, u32[]{:S(2)}) collective-permute-start(f32[1024,128]{1,0:T(8,128)} %refs_0_.1), channel_id=1, source_target_pairs={{0,4},{1,3},{2,6},{3,1},{4,0},{5,7},{6,2},{7,5},{8,12},{9,11},{10,... | collective-permute-start | bytes 1572872 | tf_op jit(solution)/shard_map/ppermute | solution.py:332
  3.7 14.8 %collective-permute-start.3 = (f32[1024,128]{1,0:T(8,128)}, f32[1024,128]{1,0:T(8,128)S(1)}, u32[]{:S(2)}, u32[]{:S(2)}) collective-permute-start(f32[1024,128]{1,0:T(8,128)} %refs_0_.1), channel_id=1, source_target_pairs={{0,2},{1,5},{2,0},{3,7},{4,6},{5,1},{6,4},{7,3},{8,10},{9,13},{10,... | collective-permute-start | bytes 1572872 | tf_op jit(solution)/shard_map/ppermute | solution.py:332
  18.0 12.0 %collective-permute-start.2 = (f32[1024,128]{1,0:T(8,128)S(1)}, f32[1024,128]{1,0:T(8,128)S(1)}, u32[]{:S(2)}, u32[]{:S(2)}) collective-permute-start(f32[1024,128]{1,0:T(8,128)S(1)} %collective-permute-done.refs_0_), channel_id=1, source_target_pairs={{0,2},{1,5},{2,0},{3,7},{4,6},{5,1},{6,4},{7,3},{8,10},{9,13},{10,... | collective-permute-start | bytes 1572872 | tf_op jit(solution)/shard_map/ppermute | solution.py:332
  18.6 11.5 %collective-permute-start.5 = (f32[1024,128]{1,0:T(8,128)S(1)}, f32[1024,128]{1,0:T(8,128)S(1)}, u32[]{:S(2)}, u32[]{:S(2)}) collective-permute-start(f32[1024,128]{1,0:T(8,128)S(1)} %collective-permute-done.refs_0_), channel_id=1, source_target_pairs={{0,1},{1,0},{2,3},{3,2},{4,5},{5,4},{6,7},{7,6},{8,9},{9,8},{10,11... | collective-permute-start | bytes 1572872 | tf_op jit(solution)/shard_map/ppermute | solution.py:335
  18.6 11.5 %collective-permute-start.6 = (f32[1024,128]{1,0:T(8,128)S(1)}, f32[1024,128]{1,0:T(8,128)S(1)}, u32[]{:S(2)}, u32[]{:S(2)}) collective-permute-start(f32[1024,128]{1,0:T(8,128)S(1)} %collective-permute-done.3.refs_1_), channel_id=1, source_target_pairs={{0,1},{1,0},{2,3},{3,2},{4,5},{5,4},{6,7},{7,6},{8,9},{9,8},{10,11... | collective-permute-start | bytes 1572872 | tf_op jit(solution)/shard_map/ppermute | solution.py:335
  30.0 11.9 %collective-permute-start.4 = (f32[1024,128]{1,0:T(8,128)S(1)}, f32[1024,128]{1,0:T(8,128)S(1)}, u32[]{:S(2)}, u32[]{:S(2)}) collective-permute-start(f32[1024,128]{1,0:T(8,128)S(1)} %collective-permute-done.2.refs_0_), channel_id=1, source_target_pairs={{0,1},{1,0},{2,3},{3,2},{4,5},{5,4},{6,7},{7,6},{8,9},{9,8},{10,11... | collective-permute-start | bytes 1572872 | tf_op jit(solution)/shard_map/ppermute | solution.py:335
  64.1 14.1 %collective-permute-start.9 = (f32[520,128]{1,0:T(8,128)S(1)}, f32[520,128]{1,0:T(8,128)S(1)}, u32[]{:S(2)}, u32[]{:S(2)}) collective-permute-start(f32[520,128]{1,0:T(8,128)S(1)} %bitcast_add_fusion.2), channel_id=1, source_target_pairs={{0,16},{8,24},{16,0},{24,8},{1,17},{9,25},{17,1},{25,9},{2,18},{10... | collective-permute-start | bytes 798728 | tf_op jit(solution)/shard_map/ppermute | solution.py:338
  66.7 11.6 %collective-permute-start.8 = (f32[520,128]{1,0:T(8,128)S(1)}, f32[520,128]{1,0:T(8,128)S(1)}, u32[]{:S(2)}, u32[]{:S(2)}) collective-permute-start(f32[520,128]{1,0:T(8,128)S(1)} %get-tuple-element.173), channel_id=1, source_target_pairs={{0,8},{8,0},{16,24},{24,16},{1,9},{9,1},{17,25},{25,17},{2,10},{10... | collective-permute-start | bytes 798728 | tf_op jit(solution)/shard_map/ppermute | solution.py:338
  78.4 12.4 %collective-permute-start.11 = (f32[512,128]{1,0:T(8,128)S(1)}, f32[512,128]{1,0:T(8,128)S(1)}, u32[]{:S(2)}, u32[]{:S(2)}) collective-permute-start(f32[512,128]{1,0:T(8,128)S(1)} %slice_add_fusion.9.refs_0_), channel_id=1, source_target_pairs={{0,8},{8,0},{16,24},{24,16},{1,9},{9,1},{17,25},{25,17},{2,10},{10... | collective-permute-start | bytes 786440 | tf_op jit(solution)/shard_map/ppermute | solution.py:338
  80.0 15.2 %collective-permute-start.10 = (f32[512,128]{1,0:T(8,128)S(1)}, f32[512,128]{1,0:T(8,128)S(1)}, u32[]{:S(2)}, u32[]{:S(2)}) collective-permute-start(f32[512,128]{1,0:T(8,128)S(1)} %slice_add_fusion.9.refs_0_), channel_id=1, source_target_pairs={{0,16},{8,24},{16,0},{24,8},{1,17},{9,25},{17,1},{25,9},{2,18},{10... | collective-permute-start | bytes 786440 | tf_op jit(solution)/shard_map/ppermute | solution.py:338
  110.1 9.3 %collective-permute-start.16 = (f32[1032,128]{1,0:T(8,128)S(1)}, f32[1032,128]{1,0:T(8,128)S(1)}, u32[]{:S(2)}, u32[]{:S(2)}) collective-permute-start(f32[1032,128]{1,0:T(8,128)S(1)} %get-tuple-element.302), channel_id=1, source_target_pairs={{0,2},{1,5},{2,0},{3,7},{4,6},{5,1},{6,4},{7,3},{8,10},{9,13},{10,... | collective-permute-start | bytes 1585160 | tf_op jit(solution)/shard_map/ppermute | solution.py:332
  114.8 13.9 %collective-permute-start.15 = (f32[1032,128]{1,0:T(8,128)S(1)}, f32[1032,128]{1,0:T(8,128)S(1)}, u32[]{:S(2)}, u32[]{:S(2)}) collective-permute-start(f32[1032,128]{1,0:T(8,128)S(1)} %get-tuple-element.301), channel_id=1, source_target_pairs={{0,2},{1,5},{2,0},{3,7},{4,6},{5,1},{6,4},{7,3},{8,10},{9,13},{10,... | collective-permute-start | bytes 1585160 | tf_op jit(solution)/shard_map/ppermute | solution.py:332
  119.5 10.3 %collective-permute-start.17 = (f32[1032,128]{1,0:T(8,128)S(1)}, f32[1032,128]{1,0:T(8,128)S(1)}, u32[]{:S(2)}, u32[]{:S(2)}) collective-permute-start(f32[1032,128]{1,0:T(8,128)S(1)} %fusion.9), channel_id=1, source_target_pairs={{0,4},{1,3},{2,6},{3,1},{4,0},{5,7},{6,2},{7,5},{8,12},{9,11},{10,... | collective-permute-start | bytes 1585160 | tf_op jit(solution)/shard_map/ppermute | solution.py:332
  130.9 9.5 %collective-permute-start.18 = (f32[1024,128]{1,0:T(8,128)S(1)}, f32[1024,128]{1,0:T(8,128)S(1)}, u32[]{:S(2)}, u32[]{:S(2)}) collective-permute-start(f32[1024,128]{1,0:T(8,128)S(1)} %slice.158.refs_0_), channel_id=1, source_target_pairs={{0,4},{1,3},{2,6},{3,1},{4,0},{5,7},{6,2},{7,5},{8,12},{9,11},{10,... | collective-permute-start | bytes 1572872 | tf_op jit(solution)/shard_map/ppermute | solution.py:332
  136.6 9.2 %collective-permute-start.21 = (f32[1024,128]{1,0:T(8,128)S(1)}, f32[1024,128]{1,0:T(8,128)S(1)}, u32[]{:S(2)}, u32[]{:S(2)}) collective-permute-start(f32[1024,128]{1,0:T(8,128)S(1)} %slice.158.refs_0_), channel_id=1, source_target_pairs={{0,2},{1,5},{2,0},{3,7},{4,6},{5,1},{6,4},{7,3},{8,10},{9,13},{10,... | collective-permute-start | bytes 1572872 | tf_op jit(solution)/shard_map/ppermute | solution.py:332
  140.4 11.0 %collective-permute-start.20 = (f32[1024,128]{1,0:T(8,128)S(1)}, f32[1024,128]{1,0:T(8,128)S(1)}, u32[]{:S(2)}, u32[]{:S(2)}) collective-permute-start(f32[1024,128]{1,0:T(8,128)S(1)} %collective-permute-done.18.refs_0_), channel_id=1, source_target_pairs={{0,2},{1,5},{2,0},{3,7},{4,6},{5,1},{6,4},{7,3},{8,10},{9,13},{10,... | collective-permute-start | bytes 1572872 | tf_op jit(solution)/shard_map/ppermute | solution.py:332
  142.0 9.4 %collective-permute-start.23 = (f32[1024,128]{1,0:T(8,128)S(1)}, f32[1024,128]{1,0:T(8,128)S(1)}, u32[]{:S(2)}, u32[]{:S(2)}) collective-permute-start(f32[1024,128]{1,0:T(8,128)S(1)} %collective-permute-done.18.refs_0_), channel_id=1, source_target_pairs={{0,1},{1,0},{2,3},{3,2},{4,5},{5,4},{6,7},{7,6},{8,9},{9,8},{10,11... | collective-permute-start | bytes 1572872 | tf_op jit(solution)/shard_map/ppermute | solution.py:335
  156.6 8.9 %collective-permute-start.25 = (f32[520,128]{1,0:T(8,128)S(1)}, f32[520,128]{1,0:T(8,128)S(1)}, u32[]{:S(2)}, u32[]{:S(2)}) collective-permute-start(f32[520,128]{1,0:T(8,128)S(1)} %slice_bitcast_fusion.5), channel_id=1, source_target_pairs={{0,8},{8,0},{16,24},{24,16},{1,9},{9,1},{17,25},{25,17},{2,10},{10... | collective-permute-start | bytes 798728 | tf_op jit(solution)/shard_map/ppermute | solution.py:338
  165.5 14.9 %collective-permute-start.27 = (f32[520,128]{1,0:T(8,128)S(1)}, f32[520,128]{1,0:T(8,128)S(1)}, u32[]{:S(2)}, u32[]{:S(2)}) collective-permute-start(f32[520,128]{1,0:T(8,128)S(1)} %bitcast_add_fusion.1), channel_id=1, source_target_pairs={{0,16},{8,24},{16,0},{24,8},{1,17},{9,25},{17,1},{25,9},{2,18},{10... | collective-permute-start | bytes 798728 | tf_op jit(solution)/shard_map/ppermute | solution.py:338
  168.3 12.2 %collective-permute-start.26 = (f32[520,128]{1,0:T(8,128)S(1)}, f32[520,128]{1,0:T(8,128)S(1)}, u32[]{:S(2)}, u32[]{:S(2)}) collective-permute-start(f32[520,128]{1,0:T(8,128)S(1)} %slice_bitcast_fusion.2), channel_id=1, source_target_pairs={{0,8},{8,0},{16,24},{24,16},{1,9},{9,1},{17,25},{25,17},{2,10},{10... | collective-permute-start | bytes 798728 | tf_op jit(solution)/shard_map/ppermute | solution.py:338
  180.6 12.5 %collective-permute-start.29 = (f32[512,128]{1,0:T(8,128)S(1)}, f32[512,128]{1,0:T(8,128)S(1)}, u32[]{:S(2)}, u32[]{:S(2)}) collective-permute-start(f32[512,128]{1,0:T(8,128)S(1)} %fusion.19.refs_0_), channel_id=1, source_target_pairs={{0,8},{8,0},{16,24},{24,16},{1,9},{9,1},{17,25},{25,17},{2,10},{10... | collective-permute-start | bytes 786440 | tf_op jit(solution)/shard_map/ppermute | solution.py:338
  182.2 17.3 %collective-permute-start.28 = (f32[512,128]{1,0:T(8,128)S(1)}, f32[512,128]{1,0:T(8,128)S(1)}, u32[]{:S(2)}, u32[]{:S(2)}) collective-permute-start(f32[512,128]{1,0:T(8,128)S(1)} %fusion.19.refs_0_), channel_id=1, source_target_pairs={{0,16},{8,24},{16,0},{24,8},{1,17},{9,25},{17,1},{25,9},{2,18},{10... | collective-permute-start | bytes 786440 | tf_op jit(solution)/shard_map/ppermute | solution.py:338
  214.8 9.3 %collective-permute-start.34 = (f32[1032,128]{1,0:T(8,128)S(1)}, f32[1032,128]{1,0:T(8,128)S(1)}, u32[]{:S(2)}, u32[]{:S(2)}) collective-permute-start(f32[1032,128]{1,0:T(8,128)S(1)} %get-tuple-element.300), channel_id=1, source_target_pairs={{0,2},{1,5},{2,0},{3,7},{4,6},{5,1},{6,4},{7,3},{8,10},{9,13},{10,... | collective-permute-start | bytes 1585160 | tf_op jit(solution)/shard_map/ppermute | solution.py:332
  219.1 14.3 %collective-permute-start.33 = (f32[1032,128]{1,0:T(8,128)S(1)}, f32[1032,128]{1,0:T(8,128)S(1)}, u32[]{:S(2)}, u32[]{:S(2)}) collective-permute-start(f32[1032,128]{1,0:T(8,128)S(1)} %get-tuple-element.299), channel_id=1, source_target_pairs={{0,2},{1,5},{2,0},{3,7},{4,6},{5,1},{6,4},{7,3},{8,10},{9,13},{10,... | collective-permute-start | bytes 1585160 | tf_op jit(solution)/shard_map/ppermute | solution.py:332
  224.2 10.2 %collective-permute-start.35 = (f32[1032,128]{1,0:T(8,128)S(1)}, f32[1032,128]{1,0:T(8,128)S(1)}, u32[]{:S(2)}, u32[]{:S(2)}) collective-permute-start(f32[1032,128]{1,0:T(8,128)S(1)} %fusion.2), channel_id=1, source_target_pairs={{0,4},{1,3},{2,6},{3,1},{4,0},{5,7},{6,2},{7,5},{8,12},{9,11},{10,... | collective-permute-start | bytes 1585160 | tf_op jit(solution)/shard_map/ppermute | solution.py:332
  235.6 9.6 %collective-permute-start.36 = (f32[1024,128]{1,0:T(8,128)S(1)}, f32[1024,128]{1,0:T(8,128)S(1)}, u32[]{:S(2)}, u32[]{:S(2)}) collective-permute-start(f32[1024,128]{1,0:T(8,128)S(1)} %slice_add_fusion.8.refs_0_), channel_id=1, source_target_pairs={{0,4},{1,3},{2,6},{3,1},{4,0},{5,7},{6,2},{7,5},{8,12},{9,11},{10,... | collective-permute-start | bytes 1572872 | tf_op jit(solution)/shard_map/ppermute | solution.py:332
  241.2 9.2 %collective-permute-start.39 = (f32[1024,128]{1,0:T(8,128)S(1)}, f32[1024,128]{1,0:T(8,128)S(1)}, u32[]{:S(2)}, u32[]{:S(2)}) collective-permute-start(f32[1024,128]{1,0:T(8,128)S(1)} %slice_add_fusion.8.refs_0_), channel_id=1, source_target_pairs={{0,2},{1,5},{2,0},{3,7},{4,6},{5,1},{6,4},{7,3},{8,10},{9,13},{10,... | collective-permute-start | bytes 1572872 | tf_op jit(solution)/shard_map/ppermute | solution.py:332
  245.2 10.9 %collective-permute-start.38 = (f32[1024,128]{1,0:T(8,128)S(1)}, f32[1024,128]{1,0:T(8,128)S(1)}, u32[]{:S(2)}, u32[]{:S(2)}) collective-permute-start(f32[1024,128]{1,0:T(8,128)S(1)} %collective-permute-done.36.refs_0_), channel_id=1, source_target_pairs={{0,2},{1,5},{2,0},{3,7},{4,6},{5,1},{6,4},{7,3},{8,10},{9,13},{10,... | collective-permute-start | bytes 1572872 | tf_op jit(solution)/shard_map/ppermute | solution.py:332
  246.8 9.3 %collective-permute-start.41 = (f32[1024,128]{1,0:T(8,128)S(1)}, f32[1024,128]{1,0:T(8,128)S(1)}, u32[]{:S(2)}, u32[]{:S(2)}) collective-permute-start(f32[1024,128]{1,0:T(8,128)S(1)} %collective-permute-done.36.refs_0_), channel_id=1, source_target_pairs={{0,1},{1,0},{2,3},{3,2},{4,5},{5,4},{6,7},{7,6},{8,9},{9,8},{10,11... | collective-permute-start | bytes 1572872 | tf_op jit(solution)/shard_map/ppermute | solution.py:335
  261.5 8.8 %collective-permute-start.43 = (f32[520,128]{1,0:T(8,128)S(1)}, f32[520,128]{1,0:T(8,128)S(1)}, u32[]{:S(2)}, u32[]{:S(2)}) collective-permute-start(f32[520,128]{1,0:T(8,128)S(1)} %slice_bitcast_fusion.4), channel_id=1, source_target_pairs={{0,8},{8,0},{16,24},{24,16},{1,9},{9,1},{17,25},{25,17},{2,10},{10... | collective-permute-start | bytes 798728 | tf_op jit(solution)/shard_map/ppermute | solution.py:338
  270.4 14.8 %collective-permute-start.45 = (f32[520,128]{1,0:T(8,128)S(1)}, f32[520,128]{1,0:T(8,128)S(1)}, u32[]{:S(2)}, u32[]{:S(2)}) collective-permute-start(f32[520,128]{1,0:T(8,128)S(1)} %bitcast_add_fusion), channel_id=1, source_target_pairs={{0,16},{8,24},{16,0},{24,8},{1,17},{9,25},{17,1},{25,9},{2,18},{10... | collective-permute-start | bytes 798728 | tf_op jit(solution)/shard_map/ppermute | solution.py:338
  273.1 12.2 %collective-permute-start.44 = (f32[520,128]{1,0:T(8,128)S(1)}, f32[520,128]{1,0:T(8,128)S(1)}, u32[]{:S(2)}, u32[]{:S(2)}) collective-permute-start(f32[520,128]{1,0:T(8,128)S(1)} %slice_bitcast_fusion), channel_id=1, source_target_pairs={{0,8},{8,0},{16,24},{24,16},{1,9},{9,1},{17,25},{25,17},{2,10},{10... | collective-permute-start | bytes 798728 | tf_op jit(solution)/shard_map/ppermute | solution.py:338
  (41 other events, 447.9 us)
